TPU v7x, 128 devices: a whole 4x4x4 slice. The times are simulated.
128 devices in a mesh: grp: 2 (over core), dev: 64 (over y, z, x).
Axes of the slice: x: 4, y: 4, z: 4, core: 2. Of those that a mesh axis runs over, the one named last changes fastest.
Arguments:
- hidden: bfloat16 [4096, 4096], P(('grp', 'dev')), may hold values from -6 to 6
- norm_gain: bfloat16 [4096], replicated, may hold values from 0.5 to 2
- expert_ids: int32 [4096, 8], P(('grp', 'dev')), may hold values from 0 to 63, all different within a row; in each aligned block of 32 rows (0 to 31, 32 to 63, ...) at most 8 rows name the same one
- gate_values: float32 [4096, 8], P(('grp', 'dev')), may hold values from 0.05 to 1
- w_gate: bfloat16 [64, 4096, 1536], P('dev', None, 'grp'), may hold values from -0.09375 to 0.09375
- w_up: bfloat16 [64, 4096, 1536], P('dev', None, 'grp'), may hold values from -0.09375 to 0.09375
- w_down: bfloat16 [64, 1536, 4096], P('dev', 'grp'), may hold values from -0.15625 to 0.15625
Outputs:
- mixed_out: bfloat16 [4096, 4096], P(('grp', 'dev'))
Inputs may be any that keep to these rules, and one draw needn't show every extreme that they name: `expert_ids`: each row names 8 different experts; no expert is named by more than 8 rows of one aligned block of 32 rows, and in every draw some expert is named by exactly 8 rows of some block.
All inputs are finite; a program needn't handle non-finite values.
Results may differ from a plain program's by a relative error of at most 0.0051.
Values may be sent and summed in bfloat16 or wider, within the bound.
A program may use at most 128 MiB of HBM per device.

v0:
```python
import jax
import jax.numpy as jnp
from jax import lax
from jax.sharding import PartitionSpec as P

D = 4096
TOP = 8


epsilon = 1e-06


def local(hidden, norm_gain, expert_ids, gate_values, w_gate, w_up, w_down):
    rows_here = hidden.shape[0]
    experts = lax.axis_size("dev")
    capacity = 2 * rows_here * TOP // experts
    hidden_f = hidden.astype(jnp.float32)
    factor = lax.rsqrt(jnp.mean(hidden_f * hidden_f, axis=1, keepdims=True) + epsilon)
    normed = (hidden_f * factor * norm_gain.astype(jnp.float32)[None, :]).astype(jnp.bfloat16)
    weights = gate_values / jnp.sum(gate_values, axis=1, keepdims=True)
    pair_expert = expert_ids.reshape(-1)
    onehot = (pair_expert[:, None] == jnp.arange(experts, dtype=jnp.int32)[None, :]).astype(
        jnp.int32
    )
    slot_index = jnp.sum((jnp.cumsum(onehot, axis=0) - onehot) * onehot, axis=1)
    target = pair_expert * capacity + slot_index
    pair_token = jnp.arange(rows_here * TOP, dtype=jnp.int32) // TOP
    buffer = jnp.zeros((experts * capacity, D), jnp.bfloat16).at[target].set(normed[pair_token])
    buffer = buffer.reshape(experts, capacity, D)
    gate_w = w_gate[0]
    up_w = w_up[0]
    down_w = w_down[0]
    doubled = jnp.concatenate([buffer, buffer], axis=0)
    received = lax.all_to_all(doubled, ("grp", "dev"), split_axis=0, concat_axis=0, tiled=True)
    sources = received.shape[0]
    flat_rows = received.reshape(-1, D)
    gate_h = jnp.dot(flat_rows, gate_w, preferred_element_type=jnp.float32)
    up_h = jnp.dot(flat_rows, up_w, preferred_element_type=jnp.float32)
    active = (jax.nn.silu(gate_h) * up_h).astype(jnp.bfloat16)
    result = jnp.dot(active, down_w, preferred_element_type=jnp.float32).astype(jnp.bfloat16)
    partial_value = result.reshape(sources, capacity, D)
    returned = lax.all_to_all(
        partial_value, ("grp", "dev"), split_axis=0, concat_axis=0, tiled=True
    )
    lower = returned[:experts].astype(jnp.float32)
    upper = returned[experts:].astype(jnp.float32)
    expert_out = (lower + upper).astype(jnp.bfloat16)
    picked = expert_out.reshape(experts * capacity, D)[target]
    contrib = (picked.astype(jnp.float32) * weights.reshape(-1)[:, None]).reshape(rows_here, TOP, D)
    return (hidden_f + jnp.sum(contrib, axis=1)).astype(jnp.bfloat16)


def solution(mesh):
    return jax.shard_map(
        local,
        mesh=mesh,
        in_specs=(
            P(("grp", "dev"), None),
            P(),
            P(("grp", "dev"), None),
            P(("grp", "dev"), None),
            P("dev", None, "grp"),
            P("dev", None, "grp"),
            P("dev", "grp", None),
        ),
        out_specs=P(("grp", "dev"), None),
        check_vma=False,
    )
```

profile of v0, /device:TPU:3, one launch (start us, length us, event | category | flops | bytes accessed | tf_op | source)
XLA Modules:
  0.0 307.3 jit_solution(1400458663200898831)
XLA Ops:
  0.0 0.8 copy.10
  0.8 0.1 eq.29
  0.9 0.1 eq.25
  0.9 0.7 broadcast_multiply_fusion
  1.7 0.6 reduce-window.6
  2.3 0.2 slice_reduce_fusion
  2.5 0.1 copy.9
  2.6 0.1 mul.56
  2.7 0.7 convert_element_type.44
  3.4 1.1 fusion.16
  4.5 0.1 fusion.22
  4.6 1.1 fusion.18
  5.7 12.1 %scatter_custom_fusion = bf16[512,4096]{1,0:T(8,128)(2,1)} fusion(s32[256]{0:T(256)S(1)} %bitcast.51, bf16[32,4096]{1,0:T(8,128)(2,1)S(1)} %fusion.18, s32[1024]{0:T(1024)S(1)} %pad_clamp_fusion.1, bf16[]{:T(256)} %constant.29.clone.1), kind=kCustom, calls=%fused_computation.17 | custom fusion | bytes 4194306 | tf_op jit(solution)/shard_map/scatter | solution.py:28
  17.8 7.4 %pad_maximum_fusion = bf16[128,8,4096]{2,1,0:T(8,128)(2,1)} fusion(bf16[64,8,4096]{2,1,0:T(8,128)(2,1)} %bitcast.49), kind=kLoop, calls=%fused_computation.3 | loop fusion | flops 4194304 | bytes 12582912 | tf_op jit(solution)/shard_map/concatenate | solution.py:33
  25.3 111.7 %all_to_all.10 = bf16[128,8,4096]{2,1,0:T(8,128)(2,1)S(1)} all-to-all(bf16[128,8,4096]{2,1,0:T(8,128)(2,1)} %pad_maximum_fusion), channel_id=1, replica_groups=mesh['grp'=2,'dev'=64] {'grp','dev'}, dimensions={0} | all-to-all | bytes 16777216 | tf_op jit(solution)/shard_map/all_to_all | solution.py:34
  137.0 9.2 %fusion = f32[1024,768]{1,0:T(8,128)S(1)} fusion(bf16[128,8,4096]{2,1,0:T(8,128)(2,1)S(1)} %all_to_all.10, bf16[1,4096,768]{2,1,0:T(8,128)(2,1)} %param.12), kind=kOutput, calls=%fused_computation.4 | convolution fusion | flops 6442450944 | bytes 17825792 | tf_op jit(solution)/shard_map/dot_general | solution.py:38
  146.2 0.0 slice-done
  146.2 0.0 slice-done.1
  146.2 0.0 slice-start.3
  146.2 7.0 %multiply_convert_fusion = bf16[1024,768]{1,0:T(8,128)(2,1)S(1)} fusion(f32[1024,768]{1,0:T(8,128)S(1)} %fusion, bf16[1,4096,768]{2,1,0:T(8,128)(2,1)S(1)} %bitcast.55, bf16[128,8,4096]{2,1,0:T(8,128)(2,1)S(1)} %all_to_all.10), kind=kOutput, calls=%fused_computation.16 | convolution fusion | flops 6447169536 | bytes 19398656 | tf_op jit(solution)/shard_map/dot_general | solution.py:37
  153.2 0.0 slice-done.2
  153.2 0.0 slice-done.3
  153.2 8.8 %convert_bitcast_fusion = bf16[128,8,4096]{2,1,0:T(8,128)(2,1)} fusion(bf16[1024,768]{1,0:T(8,128)(2,1)S(1)} %multiply_convert_fusion, bf16[1,768,4096]{2,1,0:T(8,128)(2,1)S(1)} %bitcast.57), kind=kOutput, calls=%fused_computation.9 | convolution fusion | flops 6446645248 | bytes 16252928 | tf_op jit(solution)/shard_map/dot_general | solution.py:40
  162.1 11.4 %all-to-all-start.1 = ((bf16[128,8,4096]{2,1,0:T(8,128)(2,1)}), bf16[128,8,4096]{2,1,0:T(8,128)(2,1)}, u32[]{:S(2)}, u32[]{:S(2)}) async-start(bf16[128,8,4096]{2,1,0:T(8,128)(2,1)} %convert_bitcast_fusion), calls=%async_computation.1 | async-start | bytes 16777216 | tf_op jit(solution)/shard_map/all_to_all | solution.py:42
  173.5 0.0 copy-done.1
  173.5 0.1 copy.13
  173.6 119.1 %all-to-all-done.1 = bf16[128,8,4096]{2,1,0:T(8,128)(2,1)} async-done(((bf16[128,8,4096]{2,1,0:T(8,128)(2,1)}), bf16[128,8,4096]{2,1,0:T(8,128)(2,1)}, u32[]{:S(2)}, u32[]{:S(2)}) %all-to-all-start.1) | async-done | bytes 8388640 | tf_op jit(solution)/shard_map/all_to_all | solution.py:42
  292.6 5.6 %fusion.7 = bf16[512,4096]{1,0:T(8,128)(2,1)} fusion(bf16[128,8,4096]{2,1,0:T(8,128)(2,1)} %all-to-all-done.1), kind=kLoop, calls=%fused_computation.13 | loop fusion | flops 8388608 | bytes 12582912 | tf_op jit(solution)/shard_map/reshape | solution.py:48
  298.2 6.7 %gather_fusion = bf16[256,4096]{1,0:T(8,128)(2,1)S(1)} fusion(bf16[512,4096]{1,0:T(8,128)(2,1)} %fusion.7, s32[1024]{0:T(1024)S(1)} %pad_clamp_fusion), kind=kCustom, calls=%fused_computation.1 | custom fusion | bytes 4195328 | tf_op jit(solution)/shard_map/gather | solution.py:48
  304.8 1.6 fusion.8
  306.5 0.0 copy-done
  306.5 0.8 fusion.19
  (17 shorter events, 0.1 us)
Async XLA Ops:
  25.2 120.9 %slice-start = ((s8[6291456]{0:T(1024)(128)(4,1)}), s8[4194304]{0:T(1024)(128)(4,1)S(1)}, s32[]{:S(2)}) async-start(s8[6291456]{0:T(1024)(128)(4,1)} %bitcast.54), calls=%async_computation.2 | async-start | bytes 8388608
  137.0 9.2 %slice-start.1 = ((s8[6291456]{0:T(1024)(128)(4,1)}), s8[2097152]{0:T(1024)(128)(4,1)S(1)}, s32[]{:S(2)}) async-start(s8[6291456]{0:T(1024)(128)(4,1)} %bitcast.54), calls=%async_computation.3 | async-start | bytes 4194304
  137.0 16.2 %slice-start.2 = ((s8[6291456]{0:T(1024)(128)(4,1)}), s8[4194304]{0:T(1024)(128)(4,1)S(1)}, s32[]{:S(2)}) async-start(s8[6291456]{0:T(1024)(128)(4,1)} %bitcast.56), calls=%async_computation.4 | async-start | bytes 8388608
  146.2 7.0 %slice-start.3 = ((s8[6291456]{0:T(1024)(128)(4,1)}), s8[2097152]{0:T(1024)(128)(4,1)S(1)}, s32[]{:S(2)}) async-start(s8[6291456]{0:T(1024)(128)(4,1)} %bitcast.56), calls=%async_computation.5 | async-start | bytes 4194304
  162.1 11.4 %copy-start.1 = (f32[32,8]{0,1:T(8,128)S(1)}, f32[32,8]{0,1:T(8,128)}, u32[]{:S(2)}) copy-start(f32[32,8]{0,1:T(8,128)} %param.10) | copy-start | bytes 3076
  162.1 130.6 %all-to-all-start.1 = ((bf16[128,8,4096]{2,1,0:T(8,128)(2,1)}), bf16[128,8,4096]{2,1,0:T(8,128)(2,1)}, u32[]{:S(2)}, u32[]{:S(2)}) async-start(bf16[128,8,4096]{2,1,0:T(8,128)(2,1)} %convert_bitcast_fusion), calls=%async_computation.1 | async-start | bytes 16777216 | tf_op jit(solution)/shard_map/all_to_all | solution.py:42
  298.2 8.3 %copy-start = (bf16[32,4096]{1,0:T(8,128)(2,1)S(1)}, bf16[32,4096]{1,0:T(8,128)(2,1)}, u32[]{:S(2)}) copy-start(bf16[32,4096]{1,0:T(8,128)(2,1)} %param.7) | copy-start | bytes 786436
where the time goes:
time: 308 us; the launch traced here: 307 us
  waiting for transfers between devices  119 us (39%)
  blocking collectives  112 us (36%)
  matrix products  25 us (8%)
  local copies, waits for them, and re-layouts  20.2 us (7%)
  other arithmetic  19.8 us (6%)
  starting transfers between devices  11.4 us (4%)
    all_to_all x1, waiting for transfers between devices, local(): lax.all_to_all(partial_value, ('grp', 'dev'), split_axis=0, concat_axis=0...  119 us
    all_to_all x1, blocking collectives, local(): lax.all_to_all(doubled, ('grp', 'dev'), split_axis=0, concat_axis=0, tile...  112 us
    scatter x1, local copies, waits for them, and re-layouts, local(): jnp.zeros((experts * capacity, D), jnp.bfloat16).at[target]  12.1 us
    all_to_all x1, starting transfers between devices, local(): lax.all_to_all(partial_value, ('grp', 'dev'), split_axis=0, concat_axis=0...  11.4 us
    dot_general x1, matrix products, local(): up_h = jnp.dot(flat_rows, up_w, preferred_element_type=jnp.float32)  9.16 us
    dot_general x1, matrix products, local(): jnp.dot(active, down_w, preferred_element_type=jnp.float32)  8.82 us
    concatenate x1, other arithmetic, local(): doubled = jnp.concatenate([buffer, buffer], axis=0)  7.41 us
    dot_general x1, matrix products, local(): gate_h = jnp.dot(flat_rows, gate_w, preferred_element_type=jnp.float32)  6.99 us
  transfers between devices with their start and end apart: 1, of which 1 were waited for; matrix products, arithmetic and copies ran while one was open for 0% of the time, Pallas kernels for 0%

commit v1 on v0

v1 whole, which is shorter than its diff:
```python
import functools

import jax
import jax.numpy as jnp
from jax import lax
from jax.experimental import pallas as pl
from jax.experimental.pallas import tpu as pltpu
from jax.sharding import PartitionSpec as P

D = 4096
HALF = 768
TOP = 8
ROWS = 32
EPS = 1e-06
MESH = pl.DeviceIdType.MESH
F32, BF16 = jnp.float32, jnp.bfloat16

ORDERS = (("y", "z", "x"), ("z", "x", "y"), ("x", "y", "z"))
STRIDE = {"y": 16, "z": 4, "x": 1}
COUNT = (6, 5, 5)
BASE = (0, 1536, 2816)
WIDTH = 256
UNITS = [(r, j) for j in range(6) for r in range(3) if j < COUNT[r]]
NU = len(UNITS)
GROUPS = []
for _i in range(3):
    for _r in range(3):
        _js = [j for j in (2 * _i, 2 * _i + 1) if j < COUNT[_r]]
        GROUPS.append((_r, BASE[_r] + _js[0] * WIDTH, len(_js) * WIDTH, [UNITS.index((_r, j)) for j in _js]))
FREED = max(i for i, grp in enumerate(GROUPS) if grp[0] == 0)
EARLY = 4


def tile_map(r):
    out = []
    for p in range(64):
        at = dict(zip(ORDERS[r], (p % 4, p // 4 % 4, p // 16)))
        out.append(at[ORDERS[0][2]] * 16 + at[ORDERS[0][1]] * 4 + at[ORDERS[0][0]])
    return out


def unit_lanes(q):
    r, j = UNITS[q]
    return pl.ds(BASE[r] + j * WIDTH, WIDTH)


def aligned(index, rows):
    return pl.ds(pl.multiple_of(index * rows, rows), rows)


def wait_bytes(view, sem):
    pltpu.make_async_copy(view, view, sem).wait()


def body(hidden, gain, ids, gates, w_gate, w_up, w_down, out, down_other,
         g1, g2, sel, xs, rb, ra, acc, act, w1, wd, m1, m2, pick, mix,
         recv1, recv2, recv3, recv_c, recv_b, recv_a, recv_m1, recv_m2,
         send1, send2, send3, send_c, send_b, send_a, send_m,
         w_local, w_recv, w_send, d_recv, d_local):
    grp = lax.axis_index("grp")
    dev = lax.axis_index("dev")
    at = {"y": dev // 16, "z": (dev // 4) % 4, "x": dev % 4}

    def peer(axis, shift):
        other = (at[axis] + shift) % 4
        return other, dev + (other - at[axis]) * STRIDE[axis]

    def send(src, dst, ssem, rsem, target):
        pltpu.make_async_remote_copy(
            src_ref=src, dst_ref=dst, send_sem=ssem, recv_sem=rsem,
            device_id=(grp, target), device_id_type=MESH,
        ).start()

    barrier = pltpu.get_barrier_semaphore()
    for axis in ("y", "z", "x"):
        for shift in (1, 2, 3):
            _, target = peer(axis, shift)
            pl.semaphore_signal(barrier, inc=1, device_id=(grp, target), device_id_type=MESH)
    pl.semaphore_signal(barrier, inc=1, device_id=(1 - grp, dev), device_id_type=MESH)

    for i, (r, k0, kw, _) in enumerate(GROUPS):
        rows = pl.ds(k0, kw)
        pltpu.make_async_copy(w_gate.at[rows], w1.at[rows, pl.ds(0, HALF)], w_local.at[i]).start()
        pltpu.make_async_copy(w_up.at[rows], w1.at[rows, pl.ds(2 * HALF, HALF)], w_local.at[i]).start()
    for q in range(EARLY):
        pltpu.make_async_copy(w_down.at[:, unit_lanes(q)], wd.at[pl.ds(0, HALF), pl.ds(q * WIDTH, WIDTH)],
                              d_local.at[q]).start()

    squares = jnp.zeros((ROWS, WIDTH), F32)
    for q in range(NU):
        part = hidden[:, unit_lanes(q)].astype(F32)
        squares += part * part
    factor = lax.rsqrt(jnp.sum(squares, axis=1, keepdims=True) * (1.0 / D) + EPS)
    for q, (r, _) in enumerate(UNITS):
        lanes = unit_lanes(q)
        part = hidden[:, lanes].astype(F32) * factor * gain[:, lanes].astype(F32)
        g1[aligned(at[ORDERS[r][0]], 32), lanes] = part.astype(BF16)
    gate_v = gates[...]
    weight = gate_v / jnp.sum(gate_v, axis=1, keepdims=True)
    w_hi = weight.astype(BF16).astype(F32)
    w_lo = (weight - w_hi).astype(BF16).astype(F32)
    ids_f = ids[...].astype(F32)
    lane = lax.broadcasted_iota(jnp.int32, (ROWS, 128), 1)
    meta = jnp.zeros((ROWS, 128), F32)
    for i, part in enumerate((ids_f, w_hi, w_lo)):
        for k in range(TOP):
            meta = jnp.where(lane == i * TOP + k, part[:, k:k + 1], meta)
    meta = meta.astype(BF16)
    for r in range(3):
        a = at[ORDERS[r][0]]
        m1[r, aligned(a, 32), :] = meta

    pl.semaphore_wait(barrier, 10)

    for r in range(3):
        a = at[ORDERS[r][0]]
        for shift in (1, 2, 3):
            _, target = peer(ORDERS[r][0], shift)
            view = m1.at[r, aligned(a, 32), :]
            send(view, view, send_m, recv_m1.at[r], target)
    for q, (r, _) in enumerate(UNITS):
        a = at[ORDERS[r][0]]
        for shift in (1, 2, 3):
            _, target = peer(ORDERS[r][0], shift)
            view = g1.at[aligned(a, 32), unit_lanes(q)]
            send(view, view, send1, recv1.at[q], target)

    def send_other(src, dst, rsem):
        pltpu.make_async_remote_copy(
            src_ref=src, dst_ref=dst, send_sem=w_send, recv_sem=rsem,
            device_id=(1 - grp, dev), device_id_type=MESH,
        ).start()

    for i, (r, k0, kw, _) in enumerate(GROUPS):
        rows = pl.ds(k0, kw)
        send_other(w_gate.at[rows], w1.at[rows, pl.ds(HALF, HALF)], w_recv.at[i])
        send_other(w_up.at[rows], w1.at[rows, pl.ds(3 * HALF, HALF)], w_recv.at[i])
    send_other(w_down, down_other, d_recv)

    for r in range(3):
        b = at[ORDERS[r][1]]
        wait_bytes(m1.at[r, pl.ds(0, 96), :], recv_m1.at[r])
        for shift in (1, 2, 3):
            _, target = peer(ORDERS[r][1], shift)
            send(m1.at[r], m2.at[r, aligned(b, 128), :], send_m, recv_m2.at[r], target)
        m2[r, aligned(b, 128), :] = m1[r]
    for q, (r, _) in enumerate(UNITS):
        b = at[ORDERS[r][1]]
        lanes = unit_lanes(q)
        wait_bytes(g1.at[pl.ds(0, 96), lanes], recv1.at[q])
        for shift in (1, 2, 3):
            _, target = peer(ORDERS[r][1], shift)
            send(g1.at[:, lanes], g2.at[aligned(b, 128), lanes], send2, recv2.at[q], target)
        g2[aligned(b, 128), lanes] = g1[:, lanes]

    row_s = lax.broadcasted_iota(jnp.int32, (256, 256), 0)
    col_s = lax.broadcasted_iota(jnp.int32, (256, 256), 1)
    same = row_s // 32 == col_s // 32
    upper = jnp.where(same & (row_s < col_s), 1.0, 0.0).astype(BF16)
    lower = jnp.where(lax.broadcasted_iota(jnp.int32, (ROWS, ROWS), 0) > lax.broadcasted_iota(jnp.int32, (ROWS, ROWS), 1),
                      1.0, 0.0).astype(BF16)

    def experts_of(r):
        c_axis = ORDERS[r][2]
        return [(dev + (c - at[c_axis]) * STRIDE[c_axis]).astype(F32) for c in range(4)]

    def build_pick(r):
        for half in range(2):
            meta_t = jnp.transpose(m2[r, pl.ds(half * 256, 256), :].astype(F32))
            ids_t = meta_t[0:TOP]
            sub = lax.broadcasted_iota(jnp.int32, (8, 256), 0)
            block = lax.broadcasted_iota(jnp.int32, (8, 256), 1) // 32
            present = jnp.zeros((8, 256), F32)
            for c, e in enumerate(experts_of(r)):
                one = jnp.sum(jnp.where(ids_t == e, 1.0, 0.0), axis=0, keepdims=True)
                present = jnp.where(sub == c, one, present)
            slot = jnp.dot(present.astype(BF16), upper, preferred_element_type=F32)
            spot = jnp.where(present > 0.5, block.astype(F32) * 8.0 + slot, -1.0)
            index = lax.broadcasted_iota(jnp.int32, (64, 256), 0).astype(F32)
            for c in range(4):
                pick[r, half, pl.ds(c * 64, 64), :] = jnp.where(index == spot[c:c + 1], 1.0, 0.0).astype(BF16)

    def build_mix(r):
        lanes = lax.broadcasted_iota(jnp.int32, (ROWS, 128), 1)
        spots = lax.broadcasted_iota(jnp.int32, (ROWS, 256), 1)

        def one_block(n, carry):
            half, block = n // 8, n % 8
            table = m2[r, aligned(n, ROWS), :].astype(F32)
            shifted = jnp.where(lanes < TOP, table, -1.0)
            present = jnp.zeros((ROWS, 128), F32)
            his, los = [], []
            for c, e in enumerate(experts_of(r)):
                hit = jnp.where(shifted == e, 1.0, 0.0)
                present = jnp.where(lanes == c, jnp.sum(hit, axis=1, keepdims=True), present)
                his.append(jnp.sum(pltpu.roll(hit, TOP, 1) * table, axis=1, keepdims=True))
                los.append(jnp.sum(pltpu.roll(hit, 2 * TOP, 1) * table, axis=1, keepdims=True))
            slot = jnp.dot(lower, present.astype(BF16), preferred_element_type=F32)
            spot = jnp.full((ROWS, 256), -1.0, F32)
            hi = jnp.zeros((ROWS, 256), F32)
            lo = jnp.zeros((ROWS, 256), F32)
            base = (block * 8).astype(F32)
            for c in range(4):
                mine = spots // 64 == c
                where = jnp.where(present[:, c:c + 1] > 0.5, base + slot[:, c:c + 1], -1.0)
                spot = jnp.where(mine, where, spot)
                hi = jnp.where(mine, his[c], hi)
                lo = jnp.where(mine, los[c], lo)
            fits = (spots % 64).astype(F32) == spot
            mix[r, half, 0, aligned(block, ROWS), :] = jnp.where(fits, hi, 0.0).astype(BF16)
            mix[r, half, 1, aligned(block, ROWS), :] = jnp.where(fits, lo, 0.0).astype(BF16)
            return carry

        lax.fori_loop(0, 16, one_block, 0)

    for q, (r, j) in enumerate(UNITS):
        c_at = at[ORDERS[r][2]]
        lanes = unit_lanes(q)
        if j == 0:
            wait_bytes(m2.at[r, pl.ds(0, 384), :], recv_m2.at[r])
            build_pick(r)
        wait_bytes(g2.at[pl.ds(0, 384), lanes], recv2.at[q])
        for half in range(2):
            v = jnp.dot(pick[r, half], g2[pl.ds(half * 256, 256), lanes], preferred_element_type=F32).astype(BF16)
            for c in range(4):
                sel[pl.ds(c * 128 + half * 64, 64), lanes] = v[c * 64:c * 64 + 64]
        for shift in (1, 2, 3):
            other, target = peer(ORDERS[r][2], shift)
            send(sel.at[aligned(other, 128), lanes], xs.at[aligned(c_at, 128), lanes], send3, recv3.at[q], target)
        xs[aligned(c_at, 128), lanes] = sel[aligned(c_at, 128), lanes]
    for r in range(3):
        build_mix(r)

    for i, (r, k0, kw, units) in enumerate(GROUPS):
        rows = pl.ds(k0, kw)
        for q in units:
            wait_bytes(xs.at[pl.ds(0, 384), unit_lanes(q)], recv3.at[q])
        wait_bytes(w1.at[rows, pl.ds(0, 2 * HALF)], w_local.at[i])
        wait_bytes(w1.at[rows, pl.ds(0, 2 * HALF)], w_recv.at[i])
        where = tile_map(r)

        def step(n, carry, r=r, rows=rows, first=(i == 0), where=where):
            cols = pl.ds(pl.multiple_of(n * 256, 256), 256)
            res = jnp.dot(xs[:, rows], w1[rows, cols], preferred_element_type=F32)
            if first:
                acc[:, cols] = res
            elif r == 0:
                acc[:, cols] += res
            else:
                for p in range(64):
                    acc[pl.ds(where[p] * 8, 8), cols] += res[p * 8:p * 8 + 8]
            return carry

        lax.fori_loop(0, 4 * HALF // 256, step, 0)
        if i == FREED:
            wait_bytes(down_other, d_recv)
            for q in range(EARLY):
                pltpu.make_async_copy(down_other.at[:, unit_lanes(q)],
                                      wd.at[pl.ds(HALF, HALF), pl.ds(q * WIDTH, WIDTH)], d_local.at[q]).start()
            for q in range(EARLY, NU):
                cols = pl.ds((q - EARLY) * WIDTH, WIDTH)
                pltpu.make_async_copy(w_down.at[:, unit_lanes(q)], w1.at[pl.ds(0, HALF), cols], d_local.at[q]).start()
                pltpu.make_async_copy(down_other.at[:, unit_lanes(q)], w1.at[pl.ds(HALF, HALF), cols],
                                      d_local.at[q]).start()

    def activate(n, carry):
        rows = aligned(n, 32)
        v = acc[rows, 0:2 * HALF]
        act[rows, :] = (v / (1.0 + jnp.exp(-v)) * acc[rows, 2 * HALF:4 * HALF]).astype(BF16)
        return carry

    lax.fori_loop(0, 16, activate, 0)

    wait_bytes(sel.at[pl.ds(0, 384), :], send3)
    wait_bytes(g1.at[pl.ds(0, 96), :], send1)
    wait_bytes(g2.at[pl.ds(0, 384), :], send2)

    for q, (r, j) in enumerate(UNITS):
        c_at = at[ORDERS[r][2]]
        lanes = unit_lanes(q)
        if q < EARLY:
            down = wd.at[:, pl.ds(q * WIDTH, WIDTH)]
        else:
            down = w1.at[pl.ds(0, 2 * HALF), pl.ds((q - EARLY) * WIDTH, WIDTH)]
        wait_bytes(down, d_local.at[q])
        res = jnp.dot(act[...], down[...], preferred_element_type=F32)
        where = tile_map(r)
        for p in range(0, 64, 2):
            pair = jnp.concatenate([res[where[p + i] * 8:where[p + i] * 8 + 8] for i in range(2)], axis=0)
            sel[pl.ds(p * 8, 16), lanes] = pair.astype(BF16)
        for shift in (1, 2, 3):
            other, target = peer(ORDERS[r][2], shift)
            send(sel.at[aligned(other, 128), lanes], g2.at[aligned(c_at, 128), lanes], send_c, recv_c.at[q], target)
        g2[aligned(c_at, 128), lanes] = sel[aligned(c_at, 128), lanes]

    for q, (r, j) in enumerate(UNITS):
        b = at[ORDERS[r][1]]
        lanes = unit_lanes(q)
        wait_bytes(g2.at[pl.ds(0, 384), lanes], recv_c.at[q])
        for half in range(2):
            v = jnp.concatenate([g2[pl.ds(m * 128 + half * 64, 64), lanes] for m in range(4)], axis=0)
            total = jnp.dot(mix[r, half, 0], v, preferred_element_type=F32)
            total += jnp.dot(mix[r, half, 1], v, preferred_element_type=F32)
            xs[pl.ds(half * 256, 256), lanes] = total.astype(BF16)
        for shift in (1, 2, 3):
            other, target = peer(ORDERS[r][1], shift)
            send(xs.at[aligned(other, 128), lanes], rb.at[aligned(b, 128), lanes], send_b, recv_b.at[q], target)
        rb[aligned(b, 128), lanes] = xs[aligned(b, 128), lanes]

    for q, (r, j) in enumerate(UNITS):
        a = at[ORDERS[r][0]]
        lanes = unit_lanes(q)
        wait_bytes(rb.at[pl.ds(0, 384), lanes], recv_b.at[q])
        total = rb[pl.ds(0, 128), lanes].astype(F32)
        for m in range(1, 4):
            total += rb[pl.ds(m * 128, 128), lanes].astype(F32)
        g1[:, lanes] = total.astype(BF16)
        for shift in (1, 2, 3):
            other, target = peer(ORDERS[r][0], shift)
            send(g1.at[aligned(other, 32), lanes], ra.at[aligned(a, 32), lanes], send_a, recv_a.at[q], target)
        ra[aligned(a, 32), lanes] = g1[aligned(a, 32), lanes]

    for q in range(NU):
        lanes = unit_lanes(q)
        wait_bytes(ra.at[pl.ds(0, 96), lanes], recv_a.at[q])
        total = ra[pl.ds(0, 32), lanes].astype(F32)
        for m in range(1, 4):
            total += ra[pl.ds(m * 32, 32), lanes].astype(F32)
        out[:, lanes] = (hidden[:, lanes].astype(F32) + total).astype(BF16)

    wait_bytes(m1.at[:, pl.ds(0, 96), :], send_m)
    wait_bytes(m2.at[:, pl.ds(0, 384), :], send_m)
    wait_bytes(w1.at[:, pl.ds(0, 2 * HALF)], w_send)
    wait_bytes(down_other, w_send)
    wait_bytes(sel.at[pl.ds(0, 384), :], send_c)
    wait_bytes(xs.at[pl.ds(0, 384), :], send_b)
    wait_bytes(g1.at[pl.ds(0, 96), :], send_a)


def local(hidden, norm_gain, expert_ids, gate_values, w_gate, w_up, w_down):
    vmem = pl.BlockSpec(memory_space=pltpu.VMEM)
    anywhere = pl.BlockSpec(memory_space=pl.ANY)
    dma = pltpu.SemaphoreType.DMA
    buf = pltpu.VMEM
    out, _ = pl.pallas_call(
        body,
        out_shape=(
            jax.ShapeDtypeStruct((ROWS, D), BF16),
            jax.ShapeDtypeStruct((HALF, D), BF16),
        ),
        in_specs=[vmem] * 4 + [anywhere] * 3,
        out_specs=(vmem, anywhere),
        scratch_shapes=[
            buf((128, D), BF16), buf((512, D), BF16), buf((512, D), BF16), buf((512, D), BF16),
            buf((512, D), BF16), buf((128, D), BF16),
            buf((512, 4 * HALF), F32), buf((512, 2 * HALF), BF16),
            buf((D, 4 * HALF), BF16), buf((2 * HALF, EARLY * WIDTH), BF16),
            buf((3, 128, 128), BF16), buf((3, 512, 128), BF16),
            buf((3, 2, 256, 256), BF16), buf((3, 2, 2, 256, 256), BF16),
        ] + [dma((NU,))] * 6 + [dma((3,))] * 2 + [dma] * 7 + [
            dma((len(GROUPS),)), dma((len(GROUPS),)), dma, dma, dma((NU,)),
        ],
        compiler_params=pltpu.CompilerParams(
            collective_id=0, has_side_effects=True, vmem_limit_bytes=60 * 2**20
        ),
        name="expert_layer",
    )(hidden, norm_gain.reshape(1, D), expert_ids, gate_values, w_gate[0], w_up[0], w_down[0])
    return out


def solution(mesh):
    return jax.shard_map(
        local,
        mesh=mesh,
        in_specs=(
            P(("grp", "dev"), None),
            P(),
            P(("grp", "dev"), None),
            P(("grp", "dev"), None),
            P("dev", None, "grp"),
            P("dev", None, "grp"),
            P("dev", "grp", None),
        ),
        out_specs=P(("grp", "dev"), None),
        check_vma=False,
    )
```

time: 308 us -> 144 us (0.47)
  the two profiles are of different devices: /device:TPU:3 before, /device:TPU:0 now
where the time goes in v1:
time: 144 us
  Pallas kernels  138 us (96%)
  local copies, waits for them, and re-layouts  5.7 us (4%)
    pallas_call x1, Pallas kernels, local(): pl.pallas_call(body, out_shape=(jax.ShapeDtypeStruct((ROWS, D), BF16), ja...  138 us
    unnamed x3, local copies, waits for them, and re-layouts  4.38 us

profile of v1, /device:TPU:0, one launch (start us, length us, event | category | flops | bytes accessed | tf_op | source)
XLA Modules:
  0.0 144.0 jit_solution(15885879495695865727)
XLA Ops:
  0.0 1.3 reshape.3.gain
  1.3 1.4 copy.8.ids
  2.7 1.4 copy.9.gates
  4.0 138.3 %expert_layer.1 = (bf16[32,4096]{1,0:T(8,128)(2,1)}, bf16[768,4096]{1,0:T(8,128)(2,1)}) custom-call(bf16[32,4096]{1,0:T(8,128)(2,1)} %hidden.1, bf16[1,4096]{1,0:T(2,128)(2,1)} %reshape.3.gain, s32[32,8]{1,0:T(8,128)} %copy.8.ids, f32[32,8]{1,0:T(8,128)} %copy.9.gates, bf16[4096,768]{1,0:T(8,128)(2,1)} %bitcast.3, bf16[4096,768]{1,0:T(8,128)(2,1)} %bitcast.4, ...), custom_call_target="tpu_custom_call" | custom-call | tf_op jit(solution)/shard_map/expert_layer/pallas_call | solution.py:345
  142.3 1.7 %copy.11 = bf16[32,4096]{1,0:T(8,128)(2,1)} copy(bf16[32,4096]{1,0:T(8,128)(2,1)} %get-tuple-element.6) | data formatting | bytes 524288

commit v2 on v1

--- a/solution.py
+++ b/solution.py
@@ -23,12 +23,15 @@
 UNITS = [(r, j) for j in range(6) for r in range(3) if j < COUNT[r]]
 NU = len(UNITS)
 GROUPS = []
-for _i in range(3):
-    for _r in range(3):
+for _i, _order in enumerate(((0, 1, 2), (0, 1, 2), (1, 2, 0))):
+    for _r in _order:
         _js = [j for j in (2 * _i, 2 * _i + 1) if j < COUNT[_r]]
         GROUPS.append((_r, BASE[_r] + _js[0] * WIDTH, len(_js) * WIDTH, [UNITS.index((_r, j)) for j in _js]))
-FREED = max(i for i, grp in enumerate(GROUPS) if grp[0] == 0)
+FREED = max(i for i, grp in enumerate(GROUPS) if grp[0] == 1)
+LATER = BASE[1]
 EARLY = 4
+CHUNK = 1536
+LAST = 512
 
 
 def tile_map(r):
@@ -93,19 +96,17 @@
     factor = lax.rsqrt(jnp.sum(squares, axis=1, keepdims=True) * (1.0 / D) + EPS)
     for q, (r, _) in enumerate(UNITS):
         lanes = unit_lanes(q)
-        part = hidden[:, lanes].astype(F32) * factor * gain[:, lanes].astype(F32)
+        row = (BASE[r] + UNITS[q][1] * WIDTH) // 128
+        scale = jnp.concatenate([gain[row + i:row + i + 1, :] for i in range(WIDTH // 128)], axis=1).astype(F32)
+        part = hidden[:, lanes].astype(F32) * factor * scale
         g1[aligned(at[ORDERS[r][0]], 32), lanes] = part.astype(BF16)
     gate_v = gates[...]
-    weight = gate_v / jnp.sum(gate_v, axis=1, keepdims=True)
+    weight = gate_v / jnp.sum(gate_v, axis=0, keepdims=True)
     w_hi = weight.astype(BF16).astype(F32)
-    w_lo = (weight - w_hi).astype(BF16).astype(F32)
-    ids_f = ids[...].astype(F32)
-    lane = lax.broadcasted_iota(jnp.int32, (ROWS, 128), 1)
-    meta = jnp.zeros((ROWS, 128), F32)
-    for i, part in enumerate((ids_f, w_hi, w_lo)):
-        for k in range(TOP):
-            meta = jnp.where(lane == i * TOP + k, part[:, k:k + 1], meta)
-    meta = meta.astype(BF16)
+    routing = jnp.concatenate([ids[...].astype(F32), w_hi, weight - w_hi, jnp.zeros((TOP, ROWS), F32)], axis=0)
+    eye = jnp.where(lax.broadcasted_iota(jnp.int32, (4 * TOP, 128), 0) == lax.broadcasted_iota(jnp.int32, (4 * TOP, 128), 1),
+                    1.0, 0.0).astype(BF16)
+    meta = lax.dot_general(routing.astype(BF16), eye, (((0,), (0,)), ((), ())), preferred_element_type=F32).astype(BF16)
     for r in range(3):
         a = at[ORDERS[r][0]]
         m1[r, aligned(a, 32), :] = meta
@@ -131,20 +132,15 @@
             device_id=(1 - grp, dev), device_id_type=MESH,
         ).start()
 
-    for i, (r, k0, kw, _) in enumerate(GROUPS):
-        rows = pl.ds(k0, kw)
-        send_other(w_gate.at[rows], w1.at[rows, pl.ds(HALF, HALF)], w_recv.at[i])
-        send_other(w_up.at[rows], w1.at[rows, pl.ds(3 * HALF, HALF)], w_recv.at[i])
-    send_other(w_down, down_other, d_recv)
-
-    for r in range(3):
-        b = at[ORDERS[r][1]]
-        wait_bytes(m1.at[r, pl.ds(0, 96), :], recv_m1.at[r])
-        for shift in (1, 2, 3):
-            _, target = peer(ORDERS[r][1], shift)
-            send(m1.at[r], m2.at[r, aligned(b, 128), :], send_m, recv_m2.at[r], target)
-        m2[r, aligned(b, 128), :] = m1[r]
-    for q, (r, _) in enumerate(UNITS):
+    def send_weights(i):
+        if i < len(GROUPS):
+            rows = pl.ds(GROUPS[i][1], GROUPS[i][2])
+            send_other(w_gate.at[rows], w1.at[rows, pl.ds(HALF, HALF)], w_recv.at[i])
+            send_other(w_up.at[rows], w1.at[rows, pl.ds(3 * HALF, HALF)], w_recv.at[i])
+        elif i == len(GROUPS):
+            send_other(w_down, down_other, d_recv)
+
+    for q, (r, j) in enumerate(UNITS):
         b = at[ORDERS[r][1]]
         lanes = unit_lanes(q)
         wait_bytes(g1.at[pl.ds(0, 96), lanes], recv1.at[q])
@@ -152,66 +148,47 @@
             _, target = peer(ORDERS[r][1], shift)
             send(g1.at[:, lanes], g2.at[aligned(b, 128), lanes], send2, recv2.at[q], target)
         g2[aligned(b, 128), lanes] = g1[:, lanes]
+        if j == 0:
+            wait_bytes(m1.at[r, pl.ds(0, 96), :], recv_m1.at[r])
+            for shift in (1, 2, 3):
+                _, target = peer(ORDERS[r][1], shift)
+                send(m1.at[r], m2.at[r, aligned(b, 128), :], send_m, recv_m2.at[r], target)
+            m2[r, aligned(b, 128), :] = m1[r]
+        send_weights(q)
 
     row_s = lax.broadcasted_iota(jnp.int32, (256, 256), 0)
     col_s = lax.broadcasted_iota(jnp.int32, (256, 256), 1)
-    same = row_s // 32 == col_s // 32
-    upper = jnp.where(same & (row_s < col_s), 1.0, 0.0).astype(BF16)
-    lower = jnp.where(lax.broadcasted_iota(jnp.int32, (ROWS, ROWS), 0) > lax.broadcasted_iota(jnp.int32, (ROWS, ROWS), 1),
-                      1.0, 0.0).astype(BF16)
-
-    def experts_of(r):
+    upper = jnp.where((row_s // 32 == col_s // 32) & (row_s < col_s), 1.0, 0.0).astype(BF16)
+    index = lax.broadcasted_iota(jnp.int32, (64, 256), 0).astype(F32)
+
+    def routes(r, half):
+        meta_t = jnp.transpose(m2[r, pl.ds(half * 256, 256), :].astype(F32))
+        ids_t, hi_t, lo_t = (meta_t[i * TOP:i * TOP + TOP] for i in range(3))
+        sub = lax.broadcasted_iota(jnp.int32, (8, 256), 0)
+        block = (lax.broadcasted_iota(jnp.int32, (8, 256), 1) // 32).astype(F32)
+        present = jnp.zeros((8, 256), F32)
+        terms = []
         c_axis = ORDERS[r][2]
-        return [(dev + (c - at[c_axis]) * STRIDE[c_axis]).astype(F32) for c in range(4)]
+        for c in range(4):
+            expert = (dev + (c - at[c_axis]) * STRIDE[c_axis]).astype(F32)
+            hit = ids_t == expert
+            present = jnp.where(sub == c, jnp.sum(jnp.where(hit, 1.0, 0.0), axis=0, keepdims=True), present)
+            terms.append([jnp.sum(jnp.where(hit, t, 0.0), axis=0, keepdims=True) for t in (hi_t, lo_t)])
+        slot = jnp.dot(present.astype(BF16), upper, preferred_element_type=F32)
+        return jnp.where(present > 0.5, block * 8.0 + slot, -1.0), terms
 
     def build_pick(r):
         for half in range(2):
-            meta_t = jnp.transpose(m2[r, pl.ds(half * 256, 256), :].astype(F32))
-            ids_t = meta_t[0:TOP]
-            sub = lax.broadcasted_iota(jnp.int32, (8, 256), 0)
-            block = lax.broadcasted_iota(jnp.int32, (8, 256), 1) // 32
-            present = jnp.zeros((8, 256), F32)
-            for c, e in enumerate(experts_of(r)):
-                one = jnp.sum(jnp.where(ids_t == e, 1.0, 0.0), axis=0, keepdims=True)
-                present = jnp.where(sub == c, one, present)
-            slot = jnp.dot(present.astype(BF16), upper, preferred_element_type=F32)
-            spot = jnp.where(present > 0.5, block.astype(F32) * 8.0 + slot, -1.0)
-            index = lax.broadcasted_iota(jnp.int32, (64, 256), 0).astype(F32)
+            spot, _ = routes(r, half)
             for c in range(4):
                 pick[r, half, pl.ds(c * 64, 64), :] = jnp.where(index == spot[c:c + 1], 1.0, 0.0).astype(BF16)
 
     def build_mix(r):
-        lanes = lax.broadcasted_iota(jnp.int32, (ROWS, 128), 1)
-        spots = lax.broadcasted_iota(jnp.int32, (ROWS, 256), 1)
-
-        def one_block(n, carry):
-            half, block = n // 8, n % 8
-            table = m2[r, aligned(n, ROWS), :].astype(F32)
-            shifted = jnp.where(lanes < TOP, table, -1.0)
-            present = jnp.zeros((ROWS, 128), F32)
-            his, los = [], []
-            for c, e in enumerate(experts_of(r)):
-                hit = jnp.where(shifted == e, 1.0, 0.0)
-                present = jnp.where(lanes == c, jnp.sum(hit, axis=1, keepdims=True), present)
-                his.append(jnp.sum(pltpu.roll(hit, TOP, 1) * table, axis=1, keepdims=True))
-                los.append(jnp.sum(pltpu.roll(hit, 2 * TOP, 1) * table, axis=1, keepdims=True))
-            slot = jnp.dot(lower, present.astype(BF16), preferred_element_type=F32)
-            spot = jnp.full((ROWS, 256), -1.0, F32)
-            hi = jnp.zeros((ROWS, 256), F32)
-            lo = jnp.zeros((ROWS, 256), F32)
-            base = (block * 8).astype(F32)
-            for c in range(4):
-                mine = spots // 64 == c
-                where = jnp.where(present[:, c:c + 1] > 0.5, base + slot[:, c:c + 1], -1.0)
-                spot = jnp.where(mine, where, spot)
-                hi = jnp.where(mine, his[c], hi)
-                lo = jnp.where(mine, los[c], lo)
-            fits = (spots % 64).astype(F32) == spot
-            mix[r, half, 0, aligned(block, ROWS), :] = jnp.where(fits, hi, 0.0).astype(BF16)
-            mix[r, half, 1, aligned(block, ROWS), :] = jnp.where(fits, lo, 0.0).astype(BF16)
-            return carry
-
-        lax.fori_loop(0, 16, one_block, 0)
+        for half in range(2):
+            spot, terms = routes(r, half)
+            for i in range(2):
+                table = jnp.concatenate([jnp.where(index == spot[c:c + 1], terms[c][i], 0.0) for c in range(4)], axis=0)
+                mix[r, half, i] = jnp.transpose(table).astype(BF16)
 
     for q, (r, j) in enumerate(UNITS):
         c_at = at[ORDERS[r][2]]
@@ -239,19 +216,30 @@
         wait_bytes(w1.at[rows, pl.ds(0, 2 * HALF)], w_recv.at[i])
         where = tile_map(r)
 
-        def step(n, carry, r=r, rows=rows, first=(i == 0), where=where):
-            cols = pl.ds(pl.multiple_of(n * 256, 256), 256)
-            res = jnp.dot(xs[:, rows], w1[rows, cols], preferred_element_type=F32)
-            if first:
-                acc[:, cols] = res
-            elif r == 0:
-                acc[:, cols] += res
-            else:
-                for p in range(64):
-                    acc[pl.ds(where[p] * 8, 8), cols] += res[p * 8:p * 8 + 8]
-            return carry
-
-        lax.fori_loop(0, 4 * HALF // 256, step, 0)
+        if i < len(GROUPS) - 1:
+            def step(n, carry, r=r, rows=rows, first=(i == 0), where=where):
+                cols = pl.ds(pl.multiple_of(n * CHUNK, CHUNK), CHUNK)
+                res = jnp.dot(xs[:, rows], w1[rows, cols], preferred_element_type=F32)
+                if first:
+                    acc[:, cols] = res
+                elif r == 0:
+                    acc[:, cols] += res
+                else:
+                    for p in range(64):
+                        acc[pl.ds(where[p] * 8, 8), cols] += res[p * 8:p * 8 + 8]
+                return carry
+
+            lax.fori_loop(0, 4 * HALF // CHUNK, step, 0)
+        else:
+            def last(n, carry, rows=rows):
+                at_gate = pl.ds(pl.multiple_of(n * LAST, LAST), LAST)
+                at_up = pl.ds(pl.multiple_of(2 * HALF + n * LAST, LAST), LAST)
+                v = acc[:, at_gate] + jnp.dot(xs[:, rows], w1[rows, at_gate], preferred_element_type=F32)
+                u = acc[:, at_up] + jnp.dot(xs[:, rows], w1[rows, at_up], preferred_element_type=F32)
+                act[:, at_gate] = (v / (1.0 + jnp.exp(-v)) * u).astype(BF16)
+                return carry
+
+            lax.fori_loop(0, 2 * HALF // LAST, last, 0)
         if i == FREED:
             wait_bytes(down_other, d_recv)
             for q in range(EARLY):
@@ -259,17 +247,9 @@
                                       wd.at[pl.ds(HALF, HALF), pl.ds(q * WIDTH, WIDTH)], d_local.at[q]).start()
             for q in range(EARLY, NU):
                 cols = pl.ds((q - EARLY) * WIDTH, WIDTH)
-                pltpu.make_async_copy(w_down.at[:, unit_lanes(q)], w1.at[pl.ds(0, HALF), cols], d_local.at[q]).start()
-                pltpu.make_async_copy(down_other.at[:, unit_lanes(q)], w1.at[pl.ds(HALF, HALF), cols],
+                pltpu.make_async_copy(w_down.at[:, unit_lanes(q)], w1.at[pl.ds(LATER, HALF), cols], d_local.at[q]).start()
+                pltpu.make_async_copy(down_other.at[:, unit_lanes(q)], w1.at[pl.ds(LATER + HALF, HALF), cols],
                                       d_local.at[q]).start()
-
-    def activate(n, carry):
-        rows = aligned(n, 32)
-        v = acc[rows, 0:2 * HALF]
-        act[rows, :] = (v / (1.0 + jnp.exp(-v)) * acc[rows, 2 * HALF:4 * HALF]).astype(BF16)
-        return carry
-
-    lax.fori_loop(0, 16, activate, 0)
 
     wait_bytes(sel.at[pl.ds(0, 384), :], send3)
     wait_bytes(g1.at[pl.ds(0, 96), :], send1)
@@ -281,7 +261,7 @@
         if q < EARLY:
             down = wd.at[:, pl.ds(q * WIDTH, WIDTH)]
         else:
-            down = w1.at[pl.ds(0, 2 * HALF), pl.ds((q - EARLY) * WIDTH, WIDTH)]
+            down = w1.at[pl.ds(LATER, 2 * HALF), pl.ds((q - EARLY) * WIDTH, WIDTH)]
         wait_bytes(down, d_local.at[q])
         res = jnp.dot(act[...], down[...], preferred_element_type=F32)
         where = tile_map(r)
@@ -364,7 +344,7 @@
             collective_id=0, has_side_effects=True, vmem_limit_bytes=60 * 2**20
         ),
         name="expert_layer",
-    )(hidden, norm_gain.reshape(1, D), expert_ids, gate_values, w_gate[0], w_up[0], w_down[0])
+    )(hidden, norm_gain.reshape(D // 128, 128), expert_ids.T, gate_values.T, w_gate[0], w_up[0], w_down[0])
     return out
 
 

time: 144 us -> 97.7 us (0.68)
  Pallas kernels: 138 us -> 95.8 us
  local copies, waits for them, and re-layouts: 5.7 us -> 1.67 us
    pallas_call x1, Pallas kernels: 138 us -> 95.8 us  [local(): pl.pallas_call(body, out_shape=(jax.ShapeDtypeStruct((ROWS, D), BF16), ja...]
    unnamed x3 -> x1, local copies, waits for them, and re-layouts: 4.38 us -> 1.67 us
where the time goes in v2:
time: 97.7 us; the launch traced here: 97.5 us
  Pallas kernels  95.8 us (98%)
  local copies, waits for them, and re-layouts  1.67 us (2%)
    pallas_call x1, Pallas kernels, local(): pl.pallas_call(body, out_shape=(jax.ShapeDtypeStruct((ROWS, D), BF16), ja...  95.8 us

profile of v2, /device:TPU:0, one launch (start us, length us, event | category | flops | bytes accessed | tf_op | source)
XLA Modules:
  0.0 97.5 jit_solution(7525247243675080552)
XLA Ops:
  0.0 95.8 %expert_layer.1 = (bf16[32,4096]{1,0:T(8,128)(2,1)}, bf16[768,4096]{1,0:T(8,128)(2,1)}) custom-call(bf16[32,4096]{1,0:T(8,128)(2,1)} %hidden.1, bf16[32,128]{1,0:T(8,128)(2,1)} %bitcast.9, s32[8,32]{1,0:T(8,128)} %bitcast.10, f32[8,32]{1,0:T(8,128)} %bitcast.11, bf16[4096,768]{1,0:T(8,128)(2,1)} %bitcast.6, bf16[4096,768]{1,0:T(8,128)(2,1)} %bitcast.7, ...), custom_call_target="tpu_custom_call" | custom-call | tf_op jit(solution)/shard_map/expert_layer/pallas_call | solution.py:325
  95.8 1.7 %copy.9 = bf16[32,4096]{1,0:T(8,128)(2,1)} copy(bf16[32,4096]{1,0:T(8,128)(2,1)} %get-tuple-element.6) | data formatting | bytes 524288

commit v3 on v2

--- a/solution.py
+++ b/solution.py
@@ -30,6 +30,11 @@
 FREED = max(i for i, grp in enumerate(GROUPS) if grp[0] == 1)
 LATER = BASE[1]
 EARLY = 4
+BLOCK = 1024
+BLOCK_AT = [BASE[r] + UNITS[:EARLY].count((r, 0)) * WIDTH + UNITS[:EARLY].count((r, 1)) * WIDTH for r in range(3)]
+LAG = 6
+BETWEEN = ()
+BACK = (0, 16, 32, 48, 64)
 CHUNK = 1536
 LAST = 512
 
@@ -47,6 +52,11 @@
     return pl.ds(BASE[r] + j * WIDTH, WIDTH)
 
 
+def half_lanes(q, i):
+    r, j = UNITS[q]
+    return pl.ds(BASE[r] + j * WIDTH + i * (WIDTH // 2), WIDTH // 2)
+
+
 def aligned(index, rows):
     return pl.ds(pl.multiple_of(index * rows, rows), rows)
 
@@ -56,13 +66,20 @@
 
 
 def body(hidden, gain, ids, gates, w_gate, w_up, w_down, out, down_other,
-         g1, g2, sel, xs, rb, ra, acc, act, w1, wd, m1, m2, pick, mix,
-         recv1, recv2, recv3, recv_c, recv_b, recv_a, recv_m1, recv_m2,
-         send1, send2, send3, send_c, send_b, send_a, send_m,
+         g1, g2, sel, xs, rt, rb, ra, acc, act, w1, wd, m1, m2, pick, mix,
+         recv1, recv_up, recv_dn, recv_far, recv3, recv_c, recv_t, recv_b, recv_a, send_far,
+         recv_m1, recv_m2, send1, send2, send3, send_c, send_t, send_b, send_a, send_m,
          w_local, w_recv, w_send, d_recv, d_local):
     grp = lax.axis_index("grp")
     dev = lax.axis_index("dev")
     at = {"y": dev // 16, "z": (dev // 4) % 4, "x": dev % 4}
+
+    def apart(step, q):
+        def once(_, carry):
+            step(q)
+            return carry
+
+        lax.fori_loop(0, 1 + dev // 64, once, 0)
 
     def peer(axis, shift):
         other = (at[axis] + shift) % 4
@@ -140,21 +157,38 @@
         elif i == len(GROUPS):
             send_other(w_down, down_other, d_recv)
 
-    for q, (r, j) in enumerate(UNITS):
-        b = at[ORDERS[r][1]]
+    def stage_b(q):
+        r, j = UNITS[q]
+        axis = ORDERS[r][1]
+        b = at[axis]
         lanes = unit_lanes(q)
         wait_bytes(g1.at[pl.ds(0, 96), lanes], recv1.at[q])
-        for shift in (1, 2, 3):
-            _, target = peer(ORDERS[r][1], shift)
-            send(g1.at[:, lanes], g2.at[aligned(b, 128), lanes], send2, recv2.at[q], target)
+        for shift, sem in ((1, recv_up), (3, recv_dn)):
+            _, target = peer(axis, shift)
+            send(g1.at[:, lanes], g2.at[aligned(b, 128), lanes], send2, sem.at[q], target)
         g2[aligned(b, 128), lanes] = g1[:, lanes]
         if j == 0:
             wait_bytes(m1.at[r, pl.ds(0, 96), :], recv_m1.at[r])
             for shift in (1, 2, 3):
-                _, target = peer(ORDERS[r][1], shift)
+                _, target = peer(axis, shift)
                 send(m1.at[r], m2.at[r, aligned(b, 128), :], send_m, recv_m2.at[r], target)
             m2[r, aligned(b, 128), :] = m1[r]
         send_weights(q)
+
+    def pass_on(q):
+        axis = ORDERS[UNITS[q][0]][1]
+        for i, (shift, sem) in enumerate(((1, recv_up), (3, recv_dn))):
+            came, _ = peer(axis, 4 - shift)
+            _, target = peer(axis, shift)
+            wait_bytes(g2.at[aligned(came, 128), unit_lanes(q)], sem.at[q])
+            view = g2.at[aligned(came, 128), half_lanes(q, i)]
+            send(view, view, send_far.at[q], recv_far.at[q], target)
+
+    for t in range(NU + LAG):
+        if t < NU:
+            stage_b(t)
+        if t >= LAG:
+            pass_on(t - LAG)
 
     row_s = lax.broadcasted_iota(jnp.int32, (256, 256), 0)
     col_s = lax.broadcasted_iota(jnp.int32, (256, 256), 1)
@@ -190,13 +224,16 @@
                 table = jnp.concatenate([jnp.where(index == spot[c:c + 1], terms[c][i], 0.0) for c in range(4)], axis=0)
                 mix[r, half, i] = jnp.transpose(table).astype(BF16)
 
-    for q, (r, j) in enumerate(UNITS):
+    def stage_c(q):
+        r, j = UNITS[q]
         c_at = at[ORDERS[r][2]]
+        far, _ = peer(ORDERS[r][1], 2)
         lanes = unit_lanes(q)
         if j == 0:
             wait_bytes(m2.at[r, pl.ds(0, 384), :], recv_m2.at[r])
             build_pick(r)
-        wait_bytes(g2.at[pl.ds(0, 384), lanes], recv2.at[q])
+        wait_bytes(g2.at[aligned(far, 128), lanes], recv_far.at[q])
+        wait_bytes(g2.at[aligned(far, 128), lanes], send_far.at[q])
         for half in range(2):
             v = jnp.dot(pick[r, half], g2[pl.ds(half * 256, 256), lanes], preferred_element_type=F32).astype(BF16)
             for c in range(4):
@@ -205,10 +242,9 @@
             other, target = peer(ORDERS[r][2], shift)
             send(sel.at[aligned(other, 128), lanes], xs.at[aligned(c_at, 128), lanes], send3, recv3.at[q], target)
         xs[aligned(c_at, 128), lanes] = sel[aligned(c_at, 128), lanes]
-    for r in range(3):
-        build_mix(r)
-
-    for i, (r, k0, kw, units) in enumerate(GROUPS):
+
+    def features(i):
+        r, k0, kw, units = GROUPS[i]
         rows = pl.ds(k0, kw)
         for q in units:
             wait_bytes(xs.at[pl.ds(0, 384), unit_lanes(q)], recv3.at[q])
@@ -245,24 +281,39 @@
             for q in range(EARLY):
                 pltpu.make_async_copy(down_other.at[:, unit_lanes(q)],
                                       wd.at[pl.ds(HALF, HALF), pl.ds(q * WIDTH, WIDTH)], d_local.at[q]).start()
-            for q in range(EARLY, NU):
-                cols = pl.ds((q - EARLY) * WIDTH, WIDTH)
-                pltpu.make_async_copy(w_down.at[:, unit_lanes(q)], w1.at[pl.ds(LATER, HALF), cols], d_local.at[q]).start()
-                pltpu.make_async_copy(down_other.at[:, unit_lanes(q)], w1.at[pl.ds(LATER + HALF, HALF), cols],
-                                      d_local.at[q]).start()
+            for r in (1, 2, 0):
+                theirs, cols = pl.ds(BLOCK_AT[r], BLOCK), pl.ds(r * BLOCK, BLOCK)
+                sem = d_local.at[EARLY + r]
+                pltpu.make_async_copy(w_down.at[:, theirs], w1.at[pl.ds(LATER, HALF), cols], sem).start()
+                pltpu.make_async_copy(down_other.at[:, theirs], w1.at[pl.ds(LATER + HALF, HALF), cols], sem).start()
+
+    for q in range(NU):
+        stage_c(q)
+        for i, after in enumerate(BETWEEN):
+            if q == after:
+                features(i)
+    for r in range(3):
+        build_mix(r)
+    for i in range(len(BETWEEN), len(GROUPS)):
+        features(i)
 
     wait_bytes(sel.at[pl.ds(0, 384), :], send3)
     wait_bytes(g1.at[pl.ds(0, 96), :], send1)
-    wait_bytes(g2.at[pl.ds(0, 384), :], send2)
-
-    for q, (r, j) in enumerate(UNITS):
+    wait_bytes(g2.at[pl.ds(0, 256), :], send2)
+
+    def down_c(q):
+        r, j = UNITS[q]
         c_at = at[ORDERS[r][2]]
         lanes = unit_lanes(q)
         if q < EARLY:
             down = wd.at[:, pl.ds(q * WIDTH, WIDTH)]
+            wait_bytes(down, d_local.at[q])
         else:
-            down = w1.at[pl.ds(LATER, 2 * HALF), pl.ds((q - EARLY) * WIDTH, WIDTH)]
-        wait_bytes(down, d_local.at[q])
+            block = w1.at[pl.ds(LATER, 2 * HALF), pl.ds(r * BLOCK, BLOCK)]
+            start = BASE[r] + j * WIDTH - BLOCK_AT[r]
+            down = block.at[:, pl.ds(start, WIDTH)]
+            if start == 0:
+                wait_bytes(block, d_local.at[EARLY + r])
         res = jnp.dot(act[...], down[...], preferred_element_type=F32)
         where = tile_map(r)
         for p in range(0, 64, 2):
@@ -273,8 +324,9 @@
             send(sel.at[aligned(other, 128), lanes], g2.at[aligned(c_at, 128), lanes], send_c, recv_c.at[q], target)
         g2[aligned(c_at, 128), lanes] = sel[aligned(c_at, 128), lanes]
 
-    for q, (r, j) in enumerate(UNITS):
-        b = at[ORDERS[r][1]]
+    def combine(q):
+        r, _ = UNITS[q]
+        axis = ORDERS[r][1]
         lanes = unit_lanes(q)
         wait_bytes(g2.at[pl.ds(0, 384), lanes], recv_c.at[q])
         for half in range(2):
@@ -282,17 +334,29 @@
             total = jnp.dot(mix[r, half, 0], v, preferred_element_type=F32)
             total += jnp.dot(mix[r, half, 1], v, preferred_element_type=F32)
             xs[pl.ds(half * 256, 256), lanes] = total.astype(BF16)
-        for shift in (1, 2, 3):
-            other, target = peer(ORDERS[r][1], shift)
-            send(xs.at[aligned(other, 128), lanes], rb.at[aligned(b, 128), lanes], send_b, recv_b.at[q], target)
-        rb[aligned(b, 128), lanes] = xs[aligned(b, 128), lanes]
-
-    for q, (r, j) in enumerate(UNITS):
+        far, _ = peer(axis, 2)
+        for i, shift in enumerate((1, 3)):
+            _, target = peer(axis, shift)
+            view = half_lanes(q, i)
+            send(xs.at[aligned(far, 128), view], rt.at[:, view], send_t, recv_t.at[q], target)
+
+    def join(q):
+        axis = ORDERS[UNITS[q][0]][1]
+        lanes = unit_lanes(q)
+        wait_bytes(rt.at[:, lanes], recv_t.at[q])
+        for i, shift in enumerate((1, 3)):
+            other, target = peer(axis, shift)
+            rows, view = aligned(other, 128), half_lanes(q, i)
+            xs[rows, view] = (xs[rows, view].astype(F32) + rt[:, view].astype(F32)).astype(BF16)
+            send(xs.at[rows, lanes], rb.at[pl.ds(i * 128, 128), lanes], send_b, recv_b.at[q], target)
+
+    def sum_b(q):
+        r, _ = UNITS[q]
         a = at[ORDERS[r][0]]
         lanes = unit_lanes(q)
-        wait_bytes(rb.at[pl.ds(0, 384), lanes], recv_b.at[q])
-        total = rb[pl.ds(0, 128), lanes].astype(F32)
-        for m in range(1, 4):
+        wait_bytes(rb.at[:, lanes], recv_b.at[q])
+        total = xs[aligned(at[ORDERS[r][1]], 128), lanes].astype(F32)
+        for m in range(2):
             total += rb[pl.ds(m * 128, 128), lanes].astype(F32)
         g1[:, lanes] = total.astype(BF16)
         for shift in (1, 2, 3):
@@ -300,7 +364,7 @@
             send(g1.at[aligned(other, 32), lanes], ra.at[aligned(a, 32), lanes], send_a, recv_a.at[q], target)
         ra[aligned(a, 32), lanes] = g1[aligned(a, 32), lanes]
 
-    for q in range(NU):
+    def finish(q):
         lanes = unit_lanes(q)
         wait_bytes(ra.at[pl.ds(0, 96), lanes], recv_a.at[q])
         total = ra[pl.ds(0, 32), lanes].astype(F32)
@@ -308,12 +372,18 @@
             total += ra[pl.ds(m * 32, 32), lanes].astype(F32)
         out[:, lanes] = (hidden[:, lanes].astype(F32) + total).astype(BF16)
 
+    for t in range(NU + BACK[-1]):
+        for step, late in zip((down_c, combine, join, sum_b, finish), BACK):
+            if 0 <= t - late < NU:
+                apart(step, t - late)
+
     wait_bytes(m1.at[:, pl.ds(0, 96), :], send_m)
     wait_bytes(m2.at[:, pl.ds(0, 384), :], send_m)
     wait_bytes(w1.at[:, pl.ds(0, 2 * HALF)], w_send)
     wait_bytes(down_other, w_send)
     wait_bytes(sel.at[pl.ds(0, 384), :], send_c)
-    wait_bytes(xs.at[pl.ds(0, 384), :], send_b)
+    wait_bytes(rt, send_t)
+    wait_bytes(rb, send_b)
     wait_bytes(g1.at[pl.ds(0, 96), :], send_a)
 
 
@@ -332,13 +402,13 @@
         out_specs=(vmem, anywhere),
         scratch_shapes=[
             buf((128, D), BF16), buf((512, D), BF16), buf((512, D), BF16), buf((512, D), BF16),
-            buf((512, D), BF16), buf((128, D), BF16),
+            buf((128, D), BF16), buf((256, D), BF16), buf((128, D), BF16),
             buf((512, 4 * HALF), F32), buf((512, 2 * HALF), BF16),
             buf((D, 4 * HALF), BF16), buf((2 * HALF, EARLY * WIDTH), BF16),
             buf((3, 128, 128), BF16), buf((3, 512, 128), BF16),
             buf((3, 2, 256, 256), BF16), buf((3, 2, 2, 256, 256), BF16),
-        ] + [dma((NU,))] * 6 + [dma((3,))] * 2 + [dma] * 7 + [
-            dma((len(GROUPS),)), dma((len(GROUPS),)), dma, dma, dma((NU,)),
+        ] + [dma((NU,))] * 10 + [dma((3,))] * 2 + [dma] * 8 + [
+            dma((len(GROUPS),)), dma((len(GROUPS),)), dma, dma, dma((EARLY + 3,)),
         ],
         compiler_params=pltpu.CompilerParams(
             collective_id=0, has_side_effects=True, vmem_limit_bytes=60 * 2**20

time: 97.7 us -> 90.8 us (0.929)
  Pallas kernels: 95.8 us -> 88.9 us
    pallas_call x1, Pallas kernels: 95.8 us -> 88.9 us  [local(): pl.pallas_call(body, out_shape=(jax.ShapeDtypeStruct((ROWS, D), BF16), ja...]
where the time goes in v3:
time: 90.8 us; the launch traced here: 90.6 us
  Pallas kernels  88.9 us (98%)
  local copies, waits for them, and re-layouts  1.67 us (2%)
    pallas_call x1, Pallas kernels, local(): pl.pallas_call(body, out_shape=(jax.ShapeDtypeStruct((ROWS, D), BF16), ja...  88.9 us

profile of v3, /device:TPU:0, one launch (start us, length us, event | category | flops | bytes accessed | tf_op | source)
XLA Modules:
  0.0 90.6 jit_solution(16480922447899662652)
XLA Ops:
  0.0 88.9 %expert_layer.1 = (bf16[32,4096]{1,0:T(8,128)(2,1)}, bf16[768,4096]{1,0:T(8,128)(2,1)}) custom-call(bf16[32,4096]{1,0:T(8,128)(2,1)} %hidden.1, bf16[32,128]{1,0:T(8,128)(2,1)} %bitcast.9, s32[8,32]{1,0:T(8,128)} %bitcast.10, f32[8,32]{1,0:T(8,128)} %bitcast.11, bf16[4096,768]{1,0:T(8,128)(2,1)} %bitcast.6, bf16[4096,768]{1,0:T(8,128)(2,1)} %bitcast.7, ...), custom_call_target="tpu_custom_call" | custom-call | tf_op jit(solution)/shard_map/expert_layer/pallas_call | solution.py:395
  88.9 1.7 %copy.9 = bf16[32,4096]{1,0:T(8,128)(2,1)} copy(bf16[32,4096]{1,0:T(8,128)(2,1)} %get-tuple-element.6) | data formatting | bytes 524288

commit v4 on v3

--- a/solution.py
+++ b/solution.py
@@ -32,7 +32,7 @@
 EARLY = 4
 BLOCK = 1024
 BLOCK_AT = [BASE[r] + UNITS[:EARLY].count((r, 0)) * WIDTH + UNITS[:EARLY].count((r, 1)) * WIDTH for r in range(3)]
-LAG = 6
+LAG = 16
 BETWEEN = ()
 BACK = (0, 16, 32, 48, 64)
 CHUNK = 1536

time: 90.8 us -> 89.1 us (0.981)
  Pallas kernels: 88.9 us -> 87.2 us
    pallas_call x1, Pallas kernels: 88.9 us -> 87.2 us  [local(): pl.pallas_call(body, out_shape=(jax.ShapeDtypeStruct((ROWS, D), BF16), ja...]
where the time goes in v4:
time: 89.1 us; the launch traced here: 88.9 us
  Pallas kernels  87.2 us (98%)
  local copies, waits for them, and re-layouts  1.67 us (2%)
    pallas_call x1, Pallas kernels, local(): pl.pallas_call(body, out_shape=(jax.ShapeDtypeStruct((ROWS, D), BF16), ja...  87.2 us

profile of v4, /device:TPU:0, one launch (start us, length us, event | category | flops | bytes accessed | tf_op | source)
XLA Modules:
  0.0 88.9 jit_solution(15595125917512204974)
XLA Ops:
  0.0 87.2 %expert_layer.1 = (bf16[32,4096]{1,0:T(8,128)(2,1)}, bf16[768,4096]{1,0:T(8,128)(2,1)}) custom-call(bf16[32,4096]{1,0:T(8,128)(2,1)} %hidden.1, bf16[32,128]{1,0:T(8,128)(2,1)} %bitcast.9, s32[8,32]{1,0:T(8,128)} %bitcast.10, f32[8,32]{1,0:T(8,128)} %bitcast.11, bf16[4096,768]{1,0:T(8,128)(2,1)} %bitcast.6, bf16[4096,768]{1,0:T(8,128)(2,1)} %bitcast.7, ...), custom_call_target="tpu_custom_call" | custom-call | tf_op jit(solution)/shard_map/expert_layer/pallas_call | solution.py:395
  87.2 1.7 %copy.9 = bf16[32,4096]{1,0:T(8,128)(2,1)} copy(bf16[32,4096]{1,0:T(8,128)(2,1)} %get-tuple-element.6) | data formatting | bytes 524288
